TPU v7x, 256 devices: a whole 4x4x8 slice. The times are simulated.
256 devices in a mesh: ctx: 8 (over z), expert: 32 (over y, x, core).
Axes of the slice: x: 4, y: 4, z: 8, core: 2. Of those that a mesh axis runs over, the one named last changes fastest.
Arguments:
- tokens: bfloat16 [32, 1024, 1024], P('expert', 'ctx'), may hold values from -6 to 6
- chain_ids: int32 [32, 1024], P('expert', 'ctx'), may hold values from 0 to 7, never falling along the last dimension, each value on 1 to 256 neighbouring positions
- route_ids: int32 [32, 1024, 6], P('expert', 'ctx'), may hold values from 0 to 31, all different within a row; in each aligned block of 128 rows (0 to 127, 128 to 255, ..., all dimensions but the last counted through in order) at most 32 rows name the same one
- route_weights: float32 [32, 1024, 6], P('expert', 'ctx'), may hold values from 0.1 to 0.5
- attn_gain: float32 [1024], replicated, may hold values from 0.6 to 12
- ffn_gain: float32 [1024], replicated, may hold values from 0.1 to 1.9
- chain_bias: float32 [8], replicated, may hold values from 0.5 to 2.5
- w_qkv: bfloat16 [3, 1024, 1024], P(None, 'expert', 'ctx'), may hold values from -0.1875 to 0.1875
- w_out: bfloat16 [1024, 1024], P('ctx', 'expert'), may hold values from -0.75 to 0.75
- w_gateup: bfloat16 [32, 1024, 2816], P('expert'), may hold values from -0.1875 to 0.1875
- w_down: bfloat16 [32, 1408, 1024], P('expert'), may hold values from -0.15625 to 0.15625
Outputs:
- layer_out: bfloat16 [32, 1024, 1024], P('expert', 'ctx')
Inputs may be any that keep to these rules, and one draw needn't show every extreme that they name: `route_ids`: each residue names 6 different experts. Among the 128 residues of one device (aligned blocks of the residues in order, crop after crop), no expert is named by more than 32 of them, and in every draw some expert is named by exactly 32. `chain_ids`: chain numbers never fall along a crop; a chain spans 1 to 256 residues, and some chain exactly that many.
All inputs are finite; a program needn't handle non-finite values.
Results may differ from a plain program's by a relative error of at most 0.02.
The roundings to bfloat16 on the way count: a program that leaves them out, or rounds other values in their place, can miss the bound.
Values may be sent and summed in bfloat16 or wider, within the bound.
No kernel may reach another device: no remote copies, remote signals or barrier semaphores. Data moves between devices by JAX's collectives and lax.ppermute only.
A program may use at most 64 MiB of HBM per device.

v0:
```python
import math
import jax
import jax.numpy as jnp
from jax import lax
from jax.sharding import PartitionSpec as P


def rms_scale(values, gain):
    wide = values.astype(jnp.float32)
    return wide * lax.rsqrt(jnp.mean(wide * wide, axis=-1, keepdims=True) + 1e-05) * gain


def attend(query, key, value, chains, bias):
    length = query.shape[0]
    group = bias.shape[0]
    head_dim = query.shape[1] // group
    block = min(512, length)
    scale = 1.0 / math.sqrt(head_dim)
    keys = key.reshape(length, group, head_dim)
    values = value.reshape(length, group, head_dim)
    query_blocks = query.reshape(length // block, block, group, head_dim)
    chain_blocks = chains.reshape(length // block, block)

    def one_block(items):
        q_block, c_block = items
        scores = (
            jnp.einsum("qhd,khd->hqk", q_block, keys, preferred_element_type=jnp.float32) * scale
        )
        same = (c_block[:, None] == chains[None, :]).astype(jnp.float32)
        scores = scores + bias[:, None, None] * same[None]
        top = jnp.max(scores, axis=-1, keepdims=True)
        raised = jnp.exp(scores - top)
        probs = (raised / jnp.sum(raised, axis=-1, keepdims=True)).astype(jnp.bfloat16)
        return jnp.einsum("hqk,khd->qhd", probs, values, preferred_element_type=jnp.float32).astype(
            jnp.bfloat16
        )

    return lax.map(one_block, (query_blocks, chain_blocks)).reshape(length, group * head_dim)


def per_device(
    tokens,
    chain_ids,
    route_ids,
    route_weights,
    attn_gain,
    ffn_gain,
    chain_bias,
    w_qkv,
    w_out,
    w_gateup,
    w_down,
):
    tok = tokens.shape[1]
    width = tokens.shape[2]
    inputs = tokens[0]
    normed = rms_scale(inputs, attn_gain).astype(jnp.bfloat16)
    chains = lax.all_gather(chain_ids[0], "ctx", axis=0, tiled=True)
    groups = lax.axis_size("ctx")
    per_group = chain_bias.shape[0] // groups
    bias = lax.dynamic_slice_in_dim(chain_bias, lax.axis_index("ctx") * per_group, per_group)
    qkv_columns, out_full_rows = (
        lax.all_gather(w_qkv, "ctx", axis=2, tiled=True),
        lax.all_gather(w_out, "ctx", axis=0, tiled=True),
    )
    projected = jnp.einsum(
        "tr,ird->itd",
        normed,
        lax.all_gather(qkv_columns, "expert", axis=1, tiled=True),
        preferred_element_type=jnp.float32,
    ).astype(jnp.bfloat16)
    regrouped = lax.all_to_all(projected, "ctx", split_axis=2, concat_axis=1, tiled=True)
    attended = attend(regrouped[0], regrouped[1], regrouped[2], chains, bias)
    local_rows = lax.all_to_all(attended, "ctx", split_axis=0, concat_axis=1, tiled=True)
    mixed = inputs.astype(jnp.float32) + jnp.dot(
        local_rows,
        lax.all_gather(out_full_rows, "expert", axis=1, tiled=True),
        preferred_element_type=jnp.float32,
    )
    ffn_in = rms_scale(mixed, ffn_gain).astype(jnp.bfloat16)
    held = w_gateup.shape[0]
    experts = lax.axis_size("expert") * held
    topk = route_ids.shape[2]
    cap = min(tok, tok * topk * 4 // (experts * 3))
    hidden = w_down.shape[1]
    flat_ids = route_ids[0].reshape(-1)
    onehot = (flat_ids[:, None] == jnp.arange(experts, dtype=jnp.int32)[None, :]).astype(jnp.int32)
    rank = jnp.sum((jnp.cumsum(onehot, axis=0) - onehot) * onehot, axis=1)
    slots = flat_ids * cap + rank
    select = jnp.sum(
        (
            slots.reshape(tok, topk)[:, :, None]
            == jnp.arange(experts * cap, dtype=jnp.int32)[None, None, :]
        ).astype(jnp.bfloat16),
        axis=1,
    )
    outgoing = lax.dot_general(
        select, ffn_in, (((0,), (0,)), ((), ())), preferred_element_type=jnp.float32
    )
    outgoing = outgoing.astype(jnp.bfloat16).reshape(experts, cap, width)
    block = lax.all_to_all(outgoing, "expert", split_axis=0, concat_axis=0, tiled=True)
    count = block.shape[1]
    grouped = block.reshape(-1, held, count, width)
    both = jnp.einsum("sxcd,xdf->sxcf", grouped, w_gateup, preferred_element_type=jnp.float32)
    active = (jax.nn.silu(both[..., :hidden]) * both[..., hidden:]).astype(jnp.bfloat16)
    result = jnp.einsum(
        "sxcf,xfd->sxcd", active, w_down, preferred_element_type=jnp.float32
    ).astype(jnp.bfloat16)
    returned = lax.all_to_all(
        result.reshape(-1, count, width), "expert", split_axis=0, concat_axis=0, tiled=True
    )
    picked = jnp.take(returned.reshape(-1, width), slots, axis=0).reshape(tok, topk, width)
    weights = route_weights[0]
    moe_sum = mixed
    for route in range(topk):
        moe_sum = moe_sum + weights[:, route : route + 1] * picked[:, route].astype(jnp.float32)
    return moe_sum.astype(jnp.bfloat16)[None]


def solution(mesh):
    placed = (
        P("expert", "ctx", None),
        P("expert", "ctx"),
        P("expert", "ctx", None),
        P("expert", "ctx", None),
        P(),
        P(),
        P(),
        P(None, "expert", "ctx"),
        P("ctx", "expert"),
        P("expert", None, None),
        P("expert", None, None),
    )
    return jax.shard_map(
        per_device, mesh=mesh, in_specs=placed, out_specs=P("expert", "ctx", None), check_vma=False
    )
```

profile of v0, /device:TPU:1, one launch (start us, length us, event | category | flops | bytes accessed | tf_op | source)
XLA Modules:
  0.0 299.5 jit_solution(6906347522959631811)
XLA Ops:
  6.5 23.7 %all_gather.15 = bf16[3,32,1024]{2,1,0:T(8,128)(2,1)} all-gather(bf16[3,32,128]{2,1,0:T(8,128)(2,1)} %param.20), channel_id=1, replica_groups=mesh['ctx'=8,'expert'=32] {'ctx'}, dimensions={2}, use_global_device_ids=true | all-gather | bytes 221184 | tf_op jit(solution)/shard_map/all_gather | solution.py:63
  30.3 1.1 fusion.22
  31.4 57.7 %all-gather.4.cloned.1.call-done = bf16[3,1024,1024]{2,1,0:T(8,128)(2,1)} async-done(((bf16[3,32,1024]{2,1,0:T(8,128)(2,1)}), bf16[3,1024,1024]{2,1,0:T(8,128)(2,1)}) %all-gather.4.cloned.1.call-update) | async-done | bytes 6291472 | tf_op jit(solution)/shard_map/all_gather | solution.py:69
  89.0 4.8 %fusion.21 = bf16[3,128,1024]{2,1,0:T(8,128)(2,1)} fusion(bf16[3,1024,1024]{2,1,0:T(8,128)(2,1)} %all-gather.4.cloned.1.call-done, bf16[1,128,1024]{2,1,0:T(8,128)(2,1)} %param.13, f32[1024]{0:T(1024)} %param.17, f32[128]{0:T(128)S(1)} %add_rsqrt_fusion.1), kind=kOutput, calls=%fused_computation.28 | convolution fusion | flops 806223872 | bytes 7344640 | tf_op jit(solution)/shard_map/tr,ird->itd/dot_general | solution.py:66
  93.9 2.4 copy.69
  96.3 6.7 %all-to-all-start = ((bf16[3,128,1024]{1,0,2:T(4,128)(2,1)}), bf16[3,128,1024]{1,0,2:T(4,128)(2,1)}, u32[]{:S(2)}, u32[]{:S(2)}) async-start(bf16[3,128,1024]{1,0,2:T(4,128)(2,1)} %copy.69), calls=%async_computation | async-start | bytes 2097152 | tf_op jit(solution)/shard_map/all_to_all | solution.py:72
  103.1 39.4 %all_gather.18 = bf16[1024,32]{0,1:T(8,128)(2,1)} all-gather(bf16[128,32]{0,1:T(8,128)(2,1)S(1)} %copy-done.6), channel_id=1, replica_groups=mesh['ctx'=8,'expert'=32] {'ctx'}, dimensions={0}, use_global_device_ids=true | all-gather | bytes 73728 | tf_op jit(solution)/shard_map/all_gather | solution.py:64
  142.6 0.1 copy.77
  142.7 0.1 eq.54
  142.8 0.1 reshape_squeeze.15
  143.0 11.5 %all-gather = s32[1,1024]{1,0:T(1,128)S(1)} all-gather(s32[1,128]{1,0:T(1,128)S(1)} %copy-done.9), channel_id=2, replica_groups=mesh['ctx'=8,'expert'=32] {'ctx'}, dimensions={1}, use_global_device_ids=true | all-gather | bytes 4608 | tf_op jit(solution)/shard_map/all_gather | solution.py:58
  154.5 0.5 broadcast.132
  155.0 0.7 reduce.12
  155.7 1.7 reduce-window.6
  157.4 0.3 slice_reduce_fusion
  157.7 0.6 dynamic_slice.11
  158.3 1.3 copy.70
  159.7 0.8 fusion.47
  160.5 1.8 copy.71
  162.3 0.8 copy.72
  163.1 0.8 copy.73
  164.0 8.2 %while.10 = (s32[]{:T(128)}, bf16[2,512,1,128]{3,1,2,0:T(8,128)(2,1)}, bf16[2,512,1,128]{3,1,2,0:T(8,128)(2,1)}, bf16[1024,1,128]{2,0,1:T(8,128)(2,1)}, s32[2,51...) while((s32[]{:T(128)}, ...), condition=%wide.region_4.5_spmd, body=%wide.region_1.4_spmd.sunk | while | flops 273742848 | bytes 10245305 | solution.py:38
  164.0 2.3 fusion.58
  166.3 0.5 fusion.59
  166.8 0.6 fusion.60
  167.4 0.7 copy-done.3
  168.1 2.3 fusion.58
  170.4 0.5 fusion.59
  170.9 0.6 fusion.60
  171.5 0.7 copy-done.3
  172.2 4.2 %all-to-all-start.1 = ((bf16[8,128,128]{2,1,0:T(8,128)(2,1)}), bf16[8,128,128]{2,1,0:T(8,128)(2,1)S(1)}, u32[]{:S(2)}, u32[]{:S(2)}) async-start(bf16[8,128,128]{2,1,0:T(8,128)(2,1)} %bitcast.176), calls=%async_computation.1 | async-start | bytes 524288 | tf_op jit(solution)/shard_map/all_to_all | solution.py:74
  176.5 0.1 reduce_sum.54
  176.8 1.1 fusion.20
  177.9 7.9 %all-to-all-done.1 = bf16[8,128,128]{2,1,0:T(8,128)(2,1)S(1)} async-done(((bf16[8,128,128]{2,1,0:T(8,128)(2,1)}), bf16[8,128,128]{2,1,0:T(8,128)(2,1)S(1)}, u32[]{:S(2)}, u32[]{:S(2)}) %all-to-all-start.1) | async-done | bytes 262176 | tf_op jit(solution)/shard_map/all_to_all | solution.py:74
  185.8 0.9 copy.75
  186.6 6.5 %all-gather.6.cloned.1.call-done = bf16[1024,1024]{0,1:T(8,128)(2,1)} async-done(((bf16[1024,32]{0,1:T(8,128)(2,1)}), bf16[1024,1024]{0,1:T(8,128)(2,1)}) %all-gather.6.cloned.1.call-update) | async-done | bytes 2097168 | tf_op jit(solution)/shard_map/all_gather | solution.py:77
  193.2 2.6 multiply_reduce_fusion
  195.8 0.8 convolution_convert_fusion.1
  196.6 37.6 %all_to_all.44 = bf16[32,32,1024]{2,1,0:T(8,128)(2,1)S(1)} all-to-all(bf16[32,32,1024]{2,1,0:T(8,128)(2,1)S(1)} %bitcast.172), channel_id=1, replica_groups=mesh['ctx'=8,'expert'=32] {'expert'}, dimensions={0} | all-to-all | bytes 4194304 | tf_op jit(solution)/shard_map/all_to_all | solution.py:101
  234.2 6.1 %convolution_bitcast_fusion = f32[32,1,32,2816]{3,2,0,1:T(8,128)S(1)} fusion(bf16[32,32,1024]{2,1,0:T(8,128)(2,1)S(1)} %all_to_all.44, bf16[1,1024,2816]{2,1,0:T(8,128)(2,1)S(1)} %copy-done.10), kind=kOutput, calls=%fused_computation.14 | convolution fusion | flops 5905580032 | bytes 19398656 | tf_op jit(solution)/shard_map/sxcd,xdf->sxcf/dot_general | solution.py:104
  240.4 4.8 %fusion.15 = bf16[32,32,1024]{2,1,0:T(8,128)(2,1)} fusion(bf16[1,1408,1024]{2,1,0:T(8,128)(2,1)S(1)} %copy-done, f32[32,1,32,2816]{3,2,0,1:T(8,128)S(1)} %convolution_bitcast_fusion), kind=kOutput, calls=%fused_computation.23 | convolution fusion | flops 2962489344 | bytes 16515072 | tf_op jit(solution)/shard_map/sxcf,xfd->sxcd/dot_general | solution.py:106
  245.2 4.9 %all-to-all-start.3 = ((bf16[32,32,1024]{2,1,0:T(8,128)(2,1)}), bf16[32,32,1024]{2,1,0:T(8,128)(2,1)}, u32[]{:S(2)}, u32[]{:S(2)}) async-start(bf16[32,32,1024]{2,1,0:T(8,128)(2,1)} %fusion.15), calls=%async_computation.3 | async-start | bytes 4194304 | tf_op jit(solution)/shard_map/all_to_all | solution.py:109
  250.2 0.1 mul.167
  250.4 27.6 %all-to-all-done.3 = bf16[32,32,1024]{2,1,0:T(8,128)(2,1)} async-done(((bf16[32,32,1024]{2,1,0:T(8,128)(2,1)}), bf16[32,32,1024]{2,1,0:T(8,128)(2,1)}, u32[]{:S(2)}, u32[]{:S(2)}) %all-to-all-start.3) | async-done | bytes 2097184 | tf_op jit(solution)/shard_map/all_to_all | solution.py:109
  278.0 6.4 %gather_fusion = bf16[768,1024]{1,0:T(8,128)(2,1)} fusion(bf16[1024,1024]{1,0:T(8,128)(2,1)} %bitcast.38, s32[1024]{0:T(1024)S(1)} %pad_clamp_fusion), kind=kCustom, calls=%fused_computation | custom fusion | bytes 3148800 | tf_op jit(solution)/shard_map/jit(_take)/gather | solution.py:112
  284.4 3.7 %gather.7 = bf16[128,6,1024]{2,1,0:T(8,128)(2,1)} reshape(bf16[768,1024]{1,0:T(8,128)(2,1)} %gather_fusion) | data formatting | bytes 3145728 | tf_op jit(solution)/shard_map/jit(_take)/gather | solution.py:112
  288.1 3.4 %copy_select_fusion = bf16[128,6,1024]{2,0,1:T(8,128)(2,1)S(1)} fusion(bf16[128,6,1024]{2,1,0:T(8,128)(2,1)} %gather.7, pred[128,6]{0,1:T(8,128)(4,1)S(1)} %get-tuple-element.112), kind=kLoop, calls=%fused_computation.26 | loop fusion | flops 786432 | bytes 3146496 | tf_op jit(solution)/shard_map/jit(_take)/select_n | solution.py:112
  291.6 1.1 fusion.39
  (50 shorter events, 0.5 us)
Async XLA Ops:
  6.5 233.8 %copy-start = (bf16[1,1408,1024]{2,1,0:T(8,128)(2,1)S(1)}, bf16[1,1408,1024]{2,1,0:T(8,128)(2,1)}, u32[]{:S(2)}) copy-start(bf16[1,1408,1024]{2,1,0:T(8,128)(2,1)} %param.23) | copy-start | bytes 8650756
  6.5 82.5 %all-gather.4.cloned.1.call-start = ((), (), s32[]{:S(2)}) async-start(), calls=%async_computation.4 | async-start | bytes 6488064 | tf_op jit(solution)/shard_map/all_gather | solution.py:69
  93.9 9.2 %copy-start.6 = (bf16[128,32]{0,1:T(8,128)(2,1)S(1)}, bf16[128,32]{0,1:T(8,128)(2,1)}, u32[]{:S(2)}) copy-start(bf16[128,32]{0,1:T(8,128)(2,1)} %param.21) | copy-start | bytes 24580
  93.9 48.7 %copy-start.5 = (s32[1,128,6]{1,0,2:T(1,128)S(1)}, s32[1,128,6]{1,0,2:T(1,128)}, u32[]{:S(2)}) copy-start(s32[1,128,6]{1,0,2:T(1,128)} %param.15) | copy-start | bytes 9220
  93.9 49.1 %copy-start.9 = (s32[1,128]{1,0:T(1,128)S(1)}, s32[1,128]{1,0:T(1,128)}, u32[]{:S(2)}) copy-start(s32[1,128]{1,0:T(1,128)} %param.14) | copy-start | bytes 1540
  93.9 63.8 %copy-start.11 = (f32[8]{0:T(128)S(1)}, f32[8]{0:T(128)}, u32[]{:S(2)}) copy-start(f32[8]{0:T(128)} %param.19) | copy-start | bytes 100
  96.3 62.0 %all-to-all-start = ((bf16[3,128,1024]{1,0,2:T(4,128)(2,1)}), bf16[3,128,1024]{1,0,2:T(4,128)(2,1)}, u32[]{:S(2)}, u32[]{:S(2)}) async-start(bf16[3,128,1024]{1,0,2:T(4,128)(2,1)} %copy.69), calls=%async_computation | async-start | bytes 2097152 | tf_op jit(solution)/shard_map/all_to_all | solution.py:72
  103.0 90.1 %all-gather.6.cloned.1.call-start = ((), (), s32[]{:S(2)}) async-start(), calls=%async_computation.5 | async-start | bytes 2162688 | tf_op jit(solution)/shard_map/all_gather | solution.py:77
  164.0 2.8 copy-start.2
  164.0 2.8 copy-start.4
  167.4 0.7 copy-start.3
  168.1 2.8 copy-start.2
  168.1 2.8 copy-start.4
  171.5 0.7 copy-start.3
  172.2 13.6 %all-to-all-start.1 = ((bf16[8,128,128]{2,1,0:T(8,128)(2,1)}), bf16[8,128,128]{2,1,0:T(8,128)(2,1)S(1)}, u32[]{:S(2)}, u32[]{:S(2)}) async-start(bf16[8,128,128]{2,1,0:T(8,128)(2,1)} %bitcast.176), calls=%async_computation.1 | async-start | bytes 524288 | tf_op jit(solution)/shard_map/all_to_all | solution.py:74
  176.4 19.4 %copy-start.7 = (f32[1024]{0:T(1024)S(1)}, f32[1024]{0:T(1024)}, u32[]{:S(2)}) copy-start(f32[1024]{0:T(1024)} %param.18) | copy-start | bytes 12292
  193.2 2.6 copy-start.1
  195.8 38.4 %copy-start.10 = (bf16[1,1024,2816]{2,1,0:T(8,128)(2,1)S(1)}, bf16[1,1024,2816]{2,1,0:T(8,128)(2,1)}, u32[]{:S(2)}) copy-start(bf16[1,1024,2816]{2,1,0:T(8,128)(2,1)} %param.22) | copy-start | bytes 17301508
  245.2 5.2 %copy-start.8 = (f32[1,128,6]{1,0,2:T(1,128)S(1)}, f32[1,128,6]{1,0,2:T(1,128)}, u32[]{:S(2)}) copy-start(f32[1,128,6]{1,0,2:T(1,128)} %param.16) | copy-start | bytes 9220
  245.2 32.9 %all-to-all-start.3 = ((bf16[32,32,1024]{2,1,0:T(8,128)(2,1)}), bf16[32,32,1024]{2,1,0:T(8,128)(2,1)}, u32[]{:S(2)}, u32[]{:S(2)}) async-start(bf16[32,32,1024]{2,1,0:T(8,128)(2,1)} %fusion.15), calls=%async_computation.3 | async-start | bytes 4194304 | tf_op jit(solution)/shard_map/all_to_all | solution.py:109
Sparse Core Ops, SparseCore 0:
  30.4 58.5 all-gather.3
  142.7 50.4 all-gather.5
where the time goes:
time: 300 us
  blocking collectives  112 us (37%)
  waiting for transfers between devices  99.7 us (33%)
  matrix products  24.9 us (8%)
  local copies, waits for them, and re-layouts  22.7 us (8%)
  starting transfers between devices  15.9 us (5%)
  between operations  13.6 us (5%)
  other arithmetic  10.4 us (3%)
    all_gather x1, waiting for transfers between devices, per_device(): lax.all_gather(qkv_columns, 'expert', axis=1, tiled=True)  57.7 us
    all_gather x1, blocking collectives, per_device(): lax.all_gather(w_out, 'ctx', axis=0, tiled=True)  39.4 us
    all_to_all x1, blocking collectives, per_device(): lax.all_to_all(outgoing, 'expert', split_axis=0, concat_axis=0, tiled=True)  37.6 us
    all_to_all x1, waiting for transfers between devices, per_device(): lax.all_to_all(result.reshape(-1, count, width), 'expert', split_axis=0,...  27.6 us
    all_gather x1, blocking collectives, per_device(): lax.all_gather(w_qkv, 'ctx', axis=2, tiled=True)  23.7 us
    all_gather x1, blocking collectives, per_device(): chains = lax.all_gather(chain_ids[0], 'ctx', axis=0, tiled=True)  11.5 us
    gather x2, local copies, waits for them, and re-layouts, per_device(): jnp.take(returned.reshape(-1, width), slots, axis=0)  10.1 us
    all_to_all x1, waiting for transfers between devices, per_device(): lax.all_to_all(attended, 'ctx', split_axis=0, concat_axis=1, tiled=True)  7.86 us
  transfers between devices with their start and end apart: 5, of which 4 were waited for; matrix products, arithmetic and copies ran while one was open for 7% of the time, Pallas kernels for 0%

commit v1 on v0

--- a/solution.py
+++ b/solution.py
@@ -69,7 +69,10 @@
         lax.all_gather(qkv_columns, "expert", axis=1, tiled=True),
         preferred_element_type=jnp.float32,
     ).astype(jnp.bfloat16)
-    regrouped = lax.all_to_all(projected, "ctx", split_axis=2, concat_axis=1, tiled=True)
+    n_dev = lax.axis_size("ctx")
+    pieces = jnp.stack(jnp.split(projected, n_dev, axis=2), axis=0)
+    pieces = lax.all_to_all(pieces, "ctx", split_axis=0, concat_axis=0)
+    regrouped = jnp.concatenate(pieces, axis=1)
     attended = attend(regrouped[0], regrouped[1], regrouped[2], chains, bias)
     local_rows = lax.all_to_all(attended, "ctx", split_axis=0, concat_axis=1, tiled=True)
     mixed = inputs.astype(jnp.float32) + jnp.dot(

time: 300 us -> 296 us (0.987)
  blocking collectives: 112 us -> 102 us
  waiting for transfers between devices: 99.7 us -> 104 us
    all_gather x1, blocking collectives: 39.4 us -> 33.8 us  [per_device(): lax.all_gather(w_out, 'ctx', axis=0, tiled=True)]
    all_gather x1, waiting for transfers between devices: 6.53 us -> 11.2 us  [per_device(): lax.all_gather(out_full_rows, 'expert', axis=1, tiled=True)]
    unnamed x20 -> x25, local copies, waits for them, and re-layouts: 0.15 us -> 4.75 us
    all_to_all x1, blocking collectives: 37.6 us -> 33.3 us  [per_device(): lax.all_to_all(outgoing, 'expert', split_axis=0, concat_axis=0, tiled=True)]
  transfers between devices with their start and end apart: 5 -> 5, of which waited for: 4 -> 4; matrix products, arithmetic and copies ran while one was open for 7% -> 6% of each run, Pallas kernels for 0% -> 0%
where the time goes in v1:
time: 296 us; the launch traced here: 294 us
  waiting for transfers between devices  104 us (35%)
  blocking collectives  102 us (34%)
  matrix products  27.4 us (9%)
  local copies, waits for them, and re-layouts  20.4 us (7%)
  starting transfers between devices  15.8 us (5%)
  between operations  13.7 us (5%)
  other arithmetic  10.4 us (4%)
    all_gather x1, waiting for transfers between devices, per_device(): lax.all_gather(qkv_columns, 'expert', axis=1, tiled=True)  57.7 us
    all_gather x1, blocking collectives, per_device(): lax.all_gather(w_out, 'ctx', axis=0, tiled=True)  33.8 us
    all_to_all x1, blocking collectives, per_device(): lax.all_to_all(outgoing, 'expert', split_axis=0, concat_axis=0, tiled=True)  33.3 us
    all_to_all x1, waiting for transfers between devices, per_device(): lax.all_to_all(result.reshape(-1, count, width), 'expert', split_axis=0,...  27.6 us
    all_gather x1, blocking collectives, per_device(): lax.all_gather(w_qkv, 'ctx', axis=2, tiled=True)  23.7 us
    all_gather x1, blocking collectives, per_device(): chains = lax.all_gather(chain_ids[0], 'ctx', axis=0, tiled=True)  11.5 us
    all_gather x1, waiting for transfers between devices, per_device(): lax.all_gather(out_full_rows, 'expert', axis=1, tiled=True)  11.2 us
    gather x2, local copies, waits for them, and re-layouts, per_device(): jnp.take(returned.reshape(-1, width), slots, axis=0)  10.1 us
  transfers between devices with their start and end apart: 5, of which 4 were waited for; matrix products, arithmetic and copies ran while one was open for 6% of the time, Pallas kernels for 0%

profile of v1, /device:TPU:1, one launch (start us, length us, event | category | flops | bytes accessed | tf_op | source)
XLA Modules:
  0.0 294.3 jit_solution(15124264526540278522)
XLA Ops:
  6.5 23.7 %all_gather.15 = bf16[3,32,1024]{2,1,0:T(8,128)(2,1)} all-gather(bf16[3,32,128]{2,1,0:T(8,128)(2,1)} %param.20), channel_id=1, replica_groups=mesh['ctx'=8,'expert'=32] {'ctx'}, dimensions={2}, use_global_device_ids=true | all-gather | bytes 221184 | tf_op jit(solution)/shard_map/all_gather | solution.py:63
  30.3 1.1 fusion.22
  31.4 57.7 %all-gather.4.cloned.1.call-done = bf16[3,1024,1024]{2,1,0:T(8,128)(2,1)} async-done(((bf16[3,32,1024]{2,1,0:T(8,128)(2,1)}), bf16[3,1024,1024]{2,1,0:T(8,128)(2,1)}) %all-gather.4.cloned.1.call-update) | async-done | bytes 6291472 | tf_op jit(solution)/shard_map/all_gather | solution.py:69
  89.0 3.9 %fusion.21 = bf16[3,128,1024]{2,1,0:T(8,128)(2,1)S(1)} fusion(bf16[3,1024,1024]{2,1,0:T(8,128)(2,1)} %all-gather.4.cloned.1.call-done, bf16[1,128,1024]{2,1,0:T(8,128)(2,1)} %param.13, f32[1024]{0:T(1024)} %param.17, f32[128]{0:T(128)S(1)} %add_rsqrt_fusion.1), kind=kOutput, calls=%fused_computation.28 | convolution fusion | flops 806223872 | bytes 7344640 | tf_op jit(solution)/shard_map/tr,ird->itd/dot_general | solution.py:66
  93.0 0.7 fusion.50
  93.7 0.7 fusion.49
  94.3 0.7 fusion.48
  95.0 0.7 fusion.47
  95.7 0.7 fusion.46
  96.3 0.7 fusion.45
  97.0 0.7 fusion.44
  97.6 0.7 fusion.43
  98.3 6.7 %all-to-all-start = ((bf16[8,3,128,128]{3,2,1,0:T(8,128)(2,1)}), bf16[8,3,128,128]{3,2,1,0:T(8,128)(2,1)}, u32[]{:S(2)}, u32[]{:S(2)}) async-start(bf16[8,3,128,128]{3,2,1,0:T(8,128)(2,1)} %fusion.43), calls=%async_computation | async-start | bytes 1572864 | tf_op jit(solution)/shard_map/all_to_all | solution.py:74
  105.1 33.8 %all_gather.18 = bf16[1024,32]{0,1:T(8,128)(2,1)} all-gather(bf16[128,32]{0,1:T(8,128)(2,1)S(1)} %copy-done.3), channel_id=1, replica_groups=mesh['ctx'=8,'expert'=32] {'ctx'}, dimensions={0}, use_global_device_ids=true | all-gather | bytes 73728 | tf_op jit(solution)/shard_map/all_gather | solution.py:64
  139.1 0.1 eq.54
  139.2 0.1 reshape_squeeze.15
  139.3 11.5 %all-gather = s32[1,1024]{1,0:T(1,128)S(1)} all-gather(s32[1,128]{1,0:T(1,128)S(1)} %copy-done.6), channel_id=2, replica_groups=mesh['ctx'=8,'expert'=32] {'ctx'}, dimensions={1}, use_global_device_ids=true | all-gather | bytes 4608 | tf_op jit(solution)/shard_map/all_gather | solution.py:58
  150.9 0.5 broadcast.132
  151.4 0.7 reduce.12
  152.1 1.7 reduce-window.6
  153.8 0.3 slice_reduce_fusion
  154.1 0.6 dynamic_slice.11
  154.7 1.9 fusion.55
  156.6 7.5 %while.10 = (s32[]{:T(128)}, bf16[2,512,1,128]{3,1,2,0:T(8,128)(2,1)}, bf16[2,512,1,128]{3,1,2,0:T(8,128)(2,1)}, bf16[1024,1,128]{2,0,1:T(8,128)(2,1)S(1)}, s32[...) while((s32[]{:T(128)}, ...), condition=%wide.region_4.5_spmd, body=%wide.region_1.4_spmd.sunk | while | flops 273742848 | bytes 7100001 | solution.py:38
  156.6 2.0 fusion.66
  158.6 0.5 fusion.67
  159.1 1.2 fusion.68
  160.3 2.0 fusion.66
  162.3 0.5 fusion.67
  162.9 1.2 fusion.68
  164.1 4.2 %all-to-all-start.1 = ((bf16[8,128,128]{2,1,0:T(8,128)(2,1)}), bf16[8,128,128]{2,1,0:T(8,128)(2,1)S(1)}, u32[]{:S(2)}, u32[]{:S(2)}) async-start(bf16[8,128,128]{2,1,0:T(8,128)(2,1)} %bitcast.27), calls=%async_computation.1 | async-start | bytes 524288 | tf_op jit(solution)/shard_map/all_to_all | solution.py:77
  168.4 0.1 reduce_sum.54
  168.6 1.1 fusion.20
  169.7 7.9 %all-to-all-done.1 = bf16[8,128,128]{2,1,0:T(8,128)(2,1)S(1)} async-done(((bf16[8,128,128]{2,1,0:T(8,128)(2,1)}), bf16[8,128,128]{2,1,0:T(8,128)(2,1)S(1)}, u32[]{:S(2)}, u32[]{:S(2)}) %all-to-all-start.1) | async-done | bytes 262176 | tf_op jit(solution)/shard_map/all_to_all | solution.py:77
  177.6 0.9 copy.41
  178.5 11.2 %all-gather.6.cloned.1.call-done = bf16[1024,1024]{0,1:T(8,128)(2,1)} async-done(((bf16[1024,32]{0,1:T(8,128)(2,1)}), bf16[1024,1024]{0,1:T(8,128)(2,1)}) %all-gather.6.cloned.1.call-update) | async-done | bytes 2097168 | tf_op jit(solution)/shard_map/all_gather | solution.py:80
  189.6 2.6 multiply_reduce_fusion
  192.2 0.8 convolution_convert_fusion.1
  193.0 33.3 %all_to_all.34 = bf16[32,32,1024]{2,1,0:T(8,128)(2,1)S(1)} all-to-all(bf16[32,32,1024]{2,1,0:T(8,128)(2,1)S(1)} %bitcast.202), channel_id=1, replica_groups=mesh['ctx'=8,'expert'=32] {'expert'}, dimensions={0} | all-to-all | bytes 4194304 | tf_op jit(solution)/shard_map/all_to_all | solution.py:104
  226.3 8.8 %convolution_bitcast_fusion = f32[32,1,32,2816]{3,2,0,1:T(8,128)S(1)} fusion(bf16[32,32,1024]{2,1,0:T(8,128)(2,1)S(1)} %all_to_all.34, bf16[1,1024,2816]{2,1,0:T(8,128)(2,1)} %param.22), kind=kOutput, calls=%fused_computation.14 | convolution fusion | flops 5905580032 | bytes 19398656 | tf_op jit(solution)/shard_map/sxcd,xdf->sxcf/dot_general | solution.py:107
  235.1 4.9 %fusion.15 = bf16[32,32,1024]{2,1,0:T(8,128)(2,1)} fusion(bf16[1,1408,1024]{2,1,0:T(8,128)(2,1)S(1)} %copy-done, f32[32,1,32,2816]{3,2,0,1:T(8,128)S(1)} %convolution_bitcast_fusion), kind=kOutput, calls=%fused_computation.23 | convolution fusion | flops 2962489344 | bytes 16515072 | tf_op jit(solution)/shard_map/sxcf,xfd->sxcd/dot_general | solution.py:109
  240.0 4.9 %all-to-all-start.3 = ((bf16[32,32,1024]{2,1,0:T(8,128)(2,1)}), bf16[32,32,1024]{2,1,0:T(8,128)(2,1)}, u32[]{:S(2)}, u32[]{:S(2)}) async-start(bf16[32,32,1024]{2,1,0:T(8,128)(2,1)} %fusion.15), calls=%async_computation.3 | async-start | bytes 4194304 | tf_op jit(solution)/shard_map/all_to_all | solution.py:112
  245.0 0.1 mul.167
  245.2 27.6 %all-to-all-done.3 = bf16[32,32,1024]{2,1,0:T(8,128)(2,1)} async-done(((bf16[32,32,1024]{2,1,0:T(8,128)(2,1)}), bf16[32,32,1024]{2,1,0:T(8,128)(2,1)}, u32[]{:S(2)}, u32[]{:S(2)}) %all-to-all-start.3) | async-done | bytes 2097184 | tf_op jit(solution)/shard_map/all_to_all | solution.py:112
  272.8 6.4 %gather_fusion = bf16[768,1024]{1,0:T(8,128)(2,1)} fusion(bf16[1024,1024]{1,0:T(8,128)(2,1)} %bitcast.44, s32[1024]{0:T(1024)S(1)} %pad_clamp_fusion), kind=kCustom, calls=%fused_computation | custom fusion | bytes 3148800 | tf_op jit(solution)/shard_map/jit(_take)/gather | solution.py:115
  279.2 3.7 %gather.7 = bf16[128,6,1024]{2,1,0:T(8,128)(2,1)} reshape(bf16[768,1024]{1,0:T(8,128)(2,1)} %gather_fusion) | data formatting | bytes 3145728 | tf_op jit(solution)/shard_map/jit(_take)/gather | solution.py:115
  282.9 3.4 %copy_select_fusion = bf16[128,6,1024]{2,0,1:T(8,128)(2,1)S(1)} fusion(bf16[128,6,1024]{2,1,0:T(8,128)(2,1)} %gather.7, pred[128,6]{0,1:T(8,128)(4,1)S(1)} %get-tuple-element.104), kind=kLoop, calls=%fused_computation.26 | loop fusion | flops 786432 | bytes 3146496 | tf_op jit(solution)/shard_map/jit(_take)/select_n | solution.py:115
  286.4 1.1 fusion.39
  (39 shorter events, 0.6 us)
Async XLA Ops:
  6.5 228.6 %copy-start = (bf16[1,1408,1024]{2,1,0:T(8,128)(2,1)S(1)}, bf16[1,1408,1024]{2,1,0:T(8,128)(2,1)}, u32[]{:S(2)}) copy-start(bf16[1,1408,1024]{2,1,0:T(8,128)(2,1)} %param.23) | copy-start | bytes 8650756
  6.5 82.5 %all-gather.4.cloned.1.call-start = ((), (), s32[]{:S(2)}) async-start(), calls=%async_computation.4 | async-start | bytes 6488064 | tf_op jit(solution)/shard_map/all_gather | solution.py:69
  93.0 12.1 %copy-start.3 = (bf16[128,32]{0,1:T(8,128)(2,1)S(1)}, bf16[128,32]{0,1:T(8,128)(2,1)}, u32[]{:S(2)}) copy-start(bf16[128,32]{0,1:T(8,128)(2,1)} %param.21) | copy-start | bytes 24580
  93.0 45.9 %copy-start.2 = (s32[1,128,6]{1,0,2:T(1,128)S(1)}, s32[1,128,6]{1,0,2:T(1,128)}, u32[]{:S(2)}) copy-start(s32[1,128,6]{1,0,2:T(1,128)} %param.15) | copy-start | bytes 9220
  93.0 46.3 %copy-start.6 = (s32[1,128]{1,0:T(1,128)S(1)}, s32[1,128]{1,0:T(1,128)}, u32[]{:S(2)}) copy-start(s32[1,128]{1,0:T(1,128)} %param.14) | copy-start | bytes 1540
  93.0 61.1 %copy-start.7 = (f32[8]{0:T(128)S(1)}, f32[8]{0:T(128)}, u32[]{:S(2)}) copy-start(f32[8]{0:T(128)} %param.19) | copy-start | bytes 100
  98.3 56.4 %all-to-all-start = ((bf16[8,3,128,128]{3,2,1,0:T(8,128)(2,1)}), bf16[8,3,128,128]{3,2,1,0:T(8,128)(2,1)}, u32[]{:S(2)}, u32[]{:S(2)}) async-start(bf16[8,3,128,128]{3,2,1,0:T(8,128)(2,1)} %fusion.43), calls=%async_computation | async-start | bytes 1572864 | tf_op jit(solution)/shard_map/all_to_all | solution.py:74
  105.0 84.6 %all-gather.6.cloned.1.call-start = ((), (), s32[]{:S(2)}) async-start(), calls=%async_computation.5 | async-start | bytes 2162688 | tf_op jit(solution)/shard_map/all_gather | solution.py:80
  164.1 13.5 %all-to-all-start.1 = ((bf16[8,128,128]{2,1,0:T(8,128)(2,1)}), bf16[8,128,128]{2,1,0:T(8,128)(2,1)S(1)}, u32[]{:S(2)}, u32[]{:S(2)}) async-start(bf16[8,128,128]{2,1,0:T(8,128)(2,1)} %bitcast.27), calls=%async_computation.1 | async-start | bytes 524288 | tf_op jit(solution)/shard_map/all_to_all | solution.py:77
  168.3 24.0 %copy-start.4 = (f32[1024]{0:T(1024)S(1)}, f32[1024]{0:T(1024)}, u32[]{:S(2)}) copy-start(f32[1024]{0:T(1024)} %param.18) | copy-start | bytes 12292
  189.6 2.6 copy-start.1
  240.0 5.1 %copy-start.5 = (f32[1,128,6]{1,0,2:T(1,128)S(1)}, f32[1,128,6]{1,0,2:T(1,128)}, u32[]{:S(2)}) copy-start(f32[1,128,6]{1,0,2:T(1,128)} %param.16) | copy-start | bytes 9220
  240.0 32.8 %all-to-all-start.3 = ((bf16[32,32,1024]{2,1,0:T(8,128)(2,1)}), bf16[32,32,1024]{2,1,0:T(8,128)(2,1)}, u32[]{:S(2)}, u32[]{:S(2)}) async-start(bf16[32,32,1024]{2,1,0:T(8,128)(2,1)} %fusion.15), calls=%async_computation.3 | async-start | bytes 4194304 | tf_op jit(solution)/shard_map/all_to_all | solution.py:112
Sparse Core Ops, SparseCore 0:
  30.4 58.5 all-gather.3
  139.0 50.5 all-gather.5
